TPU v7x, 32 devices: a whole 2x2x4 slice. The times are simulated.
32 devices in a mesh: dom: 8 (over y, x, core), band: 4 (over z).
Axes of the slice: x: 2, y: 2, z: 4, core: 2. Of those that a mesh axis runs over, the one named last changes fastest.
Arguments:
- waves: float32 [2048, 2048], P('dom', 'band'), may hold values from -6 to 6
- cell_matrix: float32 [64, 125, 125], P('dom')
- connect: int32 [64, 125], P('dom'), may hold values from 0 to 383, as said below
- send_index: int32 [8, 2, 64], P('dom'), may hold values from 0 to 255
- rotation: float32 [2048, 2048], P('band'), may hold values from -0.125 to 0.125
Outputs:
- rotated: float32 [2048, 2048], P('dom', 'band')
Inputs may be any that keep to these rules, and one draw needn't show every extreme that they name: On domain d, an entry of connect at or above 256 is 256 + k * 64 + s where s is below the number of slots that domain (d - 1 + 2 k) mod 8 fills on face k: exactly 64 for k = 1, between 64 // 2 (at least 1) and 64, uneven over domains, for k = 0; only those slots of send_index matter.
All inputs are finite; a program needn't handle non-finite values.
Results may differ from a plain program's by a relative error of at most 0.00012.
Values sent between devices are 32-bit elements; how exact they have to be, the bound alone decides.
A program may use at most 64 MiB of HBM per device.

v0:
```python
import functools

import jax
import jax.numpy as jnp
from jax import lax
from jax.experimental import pallas as pl
from jax.experimental.pallas import tpu as pltpu
from jax.sharding import PartitionSpec as P

DEGREE = 8
LANES = 128
MESH = pl.DeviceIdType.MESH
CUTS = 4


centre = 5.5
half_width = 9.5


def split(x):
    high = lax.reduce_precision(x, 8, 7)
    return high.astype(jnp.bfloat16), (x - high).astype(jnp.bfloat16)


def doubled(x, half):
    return x + pltpu.roll(x, half, 1)


def packed(x, half):
    high = x.astype(jnp.bfloat16)
    low = (x - high.astype(jnp.float32)).astype(jnp.bfloat16)
    lane = lax.broadcasted_iota(jnp.int32, x.shape, 1)
    return jnp.where(lane < half, high.astype(jnp.float32), low.astype(jnp.float32)).astype(
        jnp.bfloat16
    )


def mm(a, b):
    return jnp.dot(a, b, preferred_element_type=jnp.float32)


def filter_kernel(doms, owned, slots, half, high, low, pick, spread, start, out, pieces, ghosts, before, image):
    unroll = doms <= 8

    def over(body):
        if unroll:
            for d in range(doms):
                body(d)
        else:
            pl.loop(0, doms)(body)

    def begin(d):
        v = start[d]
        out[d] = v
        before[d] = jnp.zeros_like(v)
        pieces[d, :owned] = packed(v, half)

    over(begin)

    def one(step, _):
        def send(d):
            after = lax.rem(d + 1, doms) if not unroll else (d + 1) % doms
            ahead = lax.rem(d + doms - 1, doms) if not unroll else (d - 1) % doms
            g = mm(pick[d], pieces[d, :owned]).astype(jnp.bfloat16)
            pieces[after, owned : owned + slots] = g[:slots]
            pieces[ahead, owned + slots :] = g[slots:]

        over(send)

        def apply(d):
            x = pieces[d]
            y = mm(high[d], x) + mm(low[d], x)
            y = doubled(y, half)
            image[d] = y[:owned]
            after = lax.rem(d + 1, doms) if not unroll else (d + 1) % doms
            ahead = lax.rem(d + doms - 1, doms) if not unroll else (d - 1) % doms
            r = packed(y[owned:], half)
            ghosts[ahead, :slots] = r[:slots]
            ghosts[after, slots:] = r[slots:]

        over(apply)
        scale = jnp.where(step == 0, 1.0, 2.0)

        def update(d):
            y = image[d] + doubled(mm(spread[d], ghosts[d]), half)
            v = scale * y - before[d]
            before[d] = out[d]
            out[d] = v
            pieces[d, :owned] = packed(v, half)

        over(update)
        return 0

    lax.fori_loop(0, DEGREE, one, 0)


def high_low(x):
    high = x.astype(jnp.bfloat16)
    return high, (x - high.astype(jnp.float32)).astype(jnp.bfloat16)


def fused_kernel(bands, owned, slots, waves, cells, conn, send, rotation, out, *scratch):
    (acc, from_left, from_right, everyone, matrix, pick, spread, sendbuf, colrecv, pieces, ghosts,
     state, before, image, sendback, backrecv,
     z_send, z_right, z_left, m_send, m_recv, a_send, a_recv, b_send, b_recv) = scratch
    doms = 8
    width = waves.shape[1]
    size = owned + 2 * slots
    half = LANES // 2
    rows = owned // 2
    me = lax.axis_index("dom")
    z = lax.axis_index("band")
    core = lax.rem(me, 2)
    place = lax.rem(lax.div(me, 2), 2)
    upper = lax.div(me, 4)
    sib = me + 1 - 2 * core
    x_next = me + 2 - 4 * place
    y_next = me + 4 - 8 * upper
    diag = x_next + 4 - 8 * upper

    barrier = pltpu.get_barrier_semaphore()
    for t in range(1, doms):
        pl.semaphore_signal(barrier, inc=1, device_id={"dom": lax.rem(me + t, doms)}, device_id_type=MESH)

    @pl.when(z > 0)
    def _():
        pl.semaphore_signal(barrier, inc=1, device_id={"band": z - 1}, device_id_type=MESH)

    @pl.when(z < bands - 1)
    def _():
        pl.semaphore_signal(barrier, inc=1, device_id={"band": z + 1}, device_id_type=MESH)

    beside = lax.div(z + bands - 1, bands) + lax.div(2 * bands - 2 - z, bands)
    pl.semaphore_wait(barrier, doms - 1 + beside)

    cut = owned // CUTS

    def part(h):
        return pl.ds(h * cut, cut)

    def to_right(j, h):
        return pltpu.make_async_remote_copy(
            src_ref=acc.at[j, part(h)], dst_ref=from_left.at[j, part(h)], send_sem=z_send.at[j, h],
            recv_sem=z_right.at[j, h], device_id={"band": z + 1}, device_id_type=MESH)

    def to_left(j, h):
        return pltpu.make_async_remote_copy(
            src_ref=acc.at[j, part(h)], dst_ref=from_right.at[j, part(h)], send_sem=z_send.at[j, h],
            recv_sem=z_left.at[j, h], device_id={"band": z - 1}, device_id_type=MESH)

    order = []
    for r in range(bands // 2):
        order += [bands - 1 - r, r]
    w_high, w_low = high_low(waves[...])
    for j in order:
        r_high, r_low = high_low(rotation[:, j * width : (j + 1) * width])
        acc[j] = mm(w_high, r_high) + (mm(w_high, r_low) + mm(w_low, r_high))
        if j > 0:
            @pl.when(z == 0)
            def _():
                for h in range(CUTS):
                    to_right(j, h).start()
        if j < bands - 1:
            @pl.when(z == bands - 1)
            def _():
                for h in range(CUTS):
                    to_left(j, h).start()

    node = lax.broadcasted_iota(jnp.int32, (size, conn.shape[1]), 0)
    total = jnp.zeros((size, size), jnp.float32)
    for c in range(cells.shape[1]):
        seat = jnp.where(node == conn[c : c + 1, :], 1.0, 0.0).astype(jnp.bfloat16)
        a_high, a_low = high_low(cells[:, c, :])
        b_high, b_low = high_low(mm(seat, a_high) + mm(seat, a_low))
        dims = (((1,), (1,)), ((), ()))
        total = total + (
            lax.dot_general(b_high, seat, dims, preferred_element_type=jnp.float32)
            + lax.dot_general(b_low, seat, dims, preferred_element_type=jnp.float32))
    r_at = lax.broadcasted_iota(jnp.int32, (size, size), 0)
    c_at = lax.broadcasted_iota(jnp.int32, (size, size), 1)
    shift = jnp.where((r_at == c_at) & (r_at < owned), centre, 0.0)
    total = (total - shift) / half_width
    everyone[me, :rows] = total[:rows]
    everyone[me, rows:owned, rows:] = total[rows:owned, rows:]
    everyone[me, rows:owned, :rows] = total[owned:, owned:]
    everyone[me, owned:] = jnp.zeros((8, size), jnp.float32)
    everyone[me, owned : owned + 2, :slots] = send[0].astype(jnp.float32)

    def pass_on(slot, to, k):
        return pltpu.make_async_remote_copy(
            src_ref=everyone.at[slot], dst_ref=everyone.at[slot], send_sem=m_send.at[k],
            recv_sem=m_recv.at[slot], device_id={"dom": to}, device_id_type=MESH)

    sent = [pass_on(me, x_next, 0), pass_on(me, y_next, 1), pass_on(me, sib, 2)]
    for copy in sent:
        copy.start()

    def relay_right(j, at, h):
        @pl.when(z == at)
        def _():
            to_right(j, h).wait_recv()
            acc[j, part(h)] = acc[j, part(h)] + from_left[j, part(h)]
            to_right(j, h).start()

    def relay_left(j, at, h):
        @pl.when(z == at)
        def _():
            to_left(j, h).wait_recv()
            acc[j, part(h)] = acc[j, part(h)] + from_right[j, part(h)]
            to_left(j, h).start()

    for h in range(CUTS):
        relay_right(3, 1, h)
        relay_left(0, 2, h)
    pass_on(x_next, sib, 0).wait_recv()
    pass_on(y_next, sib, 0).wait_recv()
    relays = [
        pass_on(x_next * (1 - core) + y_next * core, y_next * (1 - core) + x_next * core, 3),
        pass_on(x_next, sib, 4),
        pass_on(y_next, sib, 5),
    ]
    for copy in relays:
        copy.start()
    for h in range(CUTS):
        relay_left(0, 1, h)
        relay_right(3, 2, h)
        relay_right(2, 1, h)
        relay_left(1, 2, h)
    pass_on(diag, sib, 6).wait_recv()
    last = pass_on(diag, sib, 6)
    last.start()

    lane = lax.broadcasted_iota(jnp.int32, (rows, LANES), 1)
    low_lanes = lane < half

    def prepare(d):
        upper_rows = everyone[d, :rows]
        middle = everyone[d, rows:owned]
        whole = jnp.concatenate([
            upper_rows,
            jnp.concatenate([jnp.transpose(upper_rows[:, rows:owned]), middle[:, rows:]], axis=1),
            jnp.concatenate([
                jnp.transpose(upper_rows[:, owned:]), jnp.transpose(middle[:, owned:]),
                middle[:, :rows]], axis=1)], axis=0)
        m_high, m_low = high_low(whole)
        matrix[d, :, :size] = m_high
        matrix[d, :, size:] = m_low
        tile = everyone[d, owned:, :LANES]
        other = pltpu.roll(tile, half, 1)
        first_lanes = lax.broadcasted_iota(jnp.int32, (1, LANES), 1) < half
        row = jnp.where(first_lanes, tile[0:1], other[1:2]).astype(jnp.int32)
        at = lax.broadcasted_iota(jnp.int32, (owned, LANES), 0)
        hot = jnp.where(at == row, 1.0, 0.0)
        spread[d] = hot.astype(jnp.bfloat16)
        pick[d] = jnp.transpose(hot).astype(jnp.bfloat16)

    sib_slots = [sib, x_next + 1 - 2 * core, y_next + 1 - 2 * core, diag + 1 - 2 * core]
    for slot in sib_slots:
        pass_on(slot, sib, 6).wait_recv()
    for d in range(doms):
        prepare(d)

    quarter = cut // 2
    low_quarter = lax.broadcasted_iota(jnp.int32, (quarter, LANES), 1) < half

    def exchange(t, h):
        to = lax.rem(me + t, doms)
        share = pl.ds(h * quarter, quarter)
        return pltpu.make_async_remote_copy(
            src_ref=sendbuf.at[to, share], dst_ref=colrecv.at[me, share], send_sem=a_send.at[t, h],
            recv_sem=a_recv.at[me, h], device_id={"dom": to}, device_id_type=MESH)

    def arrival(t, h):
        frm = lax.rem(me + t, doms)
        share = pl.ds(h * quarter, quarter)
        return pltpu.make_async_remote_copy(
            src_ref=sendbuf.at[frm, share], dst_ref=colrecv.at[frm, share], send_sem=a_send.at[t, h],
            recv_sem=a_recv.at[frm, h], device_id={"dom": frm}, device_id_type=MESH)

    finished = acc.at[z]
    for h in range(CUTS):
        for j in range(bands):
            if j > 0:
                @pl.when(z == j)
                def _():
                    to_right(j, h).wait_recv()
                    acc[j, part(h)] = acc[j, part(h)] + from_left[j, part(h)]
            if j < bands - 1:
                @pl.when(z == j)
                def _():
                    to_left(j, h).wait_recv()
                    acc[j, part(h)] = acc[j, part(h)] + from_right[j, part(h)]
        first, second = h * cut, h * cut + quarter
        to_rows = slice(h * quarter, (h + 1) * quarter)
        for p in range(doms // 2):
            columns = slice(p * LANES, (p + 1) * LANES)
            top = finished[first:second, columns]
            bottom = finished[second : second + quarter, columns]
            sendbuf[2 * p, to_rows] = jnp.where(low_quarter, top, pltpu.roll(bottom, half, 1))
            sendbuf[2 * p + 1, to_rows] = jnp.where(low_quarter, pltpu.roll(top, half, 1), bottom)
        for t in range(1, doms):
            exchange(t, h).start()
    colrecv[me] = sendbuf[me]
    for h in range(CUTS):
        for t in range(1, doms):
            arrival(t, h).wait_recv()

    def put(d, v):
        x = packed(v, half)
        pieces[d, :owned] = x
        pieces[d, size : size + owned] = x

    for d in range(doms):
        blk = colrecv[d]
        turned = pltpu.roll(blk, half, 1)
        left, right = jnp.where(low_lanes, blk, turned), jnp.where(low_lanes, turned, blk)
        sides = []
        for h in range(CUTS):
            at = slice(h * quarter, (h + 1) * quarter)
            sides += [left[at], right[at]]
        v = jnp.concatenate(sides, axis=0)
        state[d] = v
        before[d] = jnp.zeros_like(v)
        put(d, v)

    def spread_step():
        for d in range(doms):
            after, ahead = (d + 1) % doms, (d - 1) % doms
            g = mm(pick[d], pieces[d, :owned]).astype(jnp.bfloat16)
            for base in (0, size):
                pieces[after, base + owned : base + owned + slots] = g[:slots]
                pieces[ahead, base + owned + slots : base + size] = g[slots:]
        for d in range(doms):
            after, ahead = (d + 1) % doms, (d - 1) % doms
            y = doubled(mm(matrix[d], pieces[d]), half)
            image[d] = y[:owned]
            r = packed(y[owned:], half)
            ghosts[ahead, :slots] = r[:slots]
            ghosts[after, slots:] = r[slots:]

    def following(d, scale):
        y = image[d] + doubled(mm(spread[d], ghosts[d]), half)
        return scale * y - before[d]

    def one(step, _):
        spread_step()
        scale = jnp.where(step == 0, 1.0, 2.0)
        for d in range(doms):
            v = following(d, scale)
            before[d] = state[d]
            state[d] = v
            put(d, v)
        return 0

    lax.fori_loop(0, DEGREE - 1, one, 0)
    spread_step()

    def give(d):
        return pltpu.make_async_remote_copy(
            src_ref=sendback.at[d], dst_ref=backrecv.at[me], send_sem=b_send.at[d],
            recv_sem=b_recv.at[me], device_id={"dom": d}, device_id_type=MESH)

    for d in range(doms):
        v = following(d, 2.0)
        sendback[d] = jnp.where(low_lanes, v[:rows], v[rows:])

        @pl.when(me != d)
        def _():
            give(d).start()

    backrecv[me] = sendback[me]
    for d in range(doms):
        @pl.when(me != d)
        def _():
            pltpu.make_async_remote_copy(
                src_ref=sendback.at[d], dst_ref=backrecv.at[d], send_sem=b_send.at[d],
                recv_sem=b_recv.at[d], device_id={"dom": d}, device_id_type=MESH).wait_recv()

    for p in range(doms // 2):
        even, odd = backrecv[2 * p], backrecv[2 * p + 1]
        columns = slice(p * LANES, (p + 1) * LANES)
        out[:rows, columns] = jnp.where(low_lanes, even, pltpu.roll(odd, half, 1))
        out[rows:, columns] = jnp.where(low_lanes, pltpu.roll(even, half, 1), odd)

    for copy in sent + relays + [last]:
        copy.wait_send()
    for t in range(1, doms):
        for h in range(CUTS):
            exchange(t, h).wait_send()
    for d in range(doms):
        @pl.when(me != d)
        def _():
            give(d).wait_send()
    for j in range(bands):
        for h in range(CUTS):
            @pl.when(z < j)
            def _():
                to_right(j, h).wait_send()

            @pl.when(z > j)
            def _():
                to_left(j, h).wait_send()


def fused(waves, cell_matrix, connect, send_index, rotation):
    owned, width = waves.shape
    slots = send_index.shape[2]
    bands = lax.axis_size("band")
    size = owned + 2 * slots
    rows = owned // 2
    doms = 8
    vmem = pl.BlockSpec(memory_space=pltpu.VMEM)
    f32, b16 = jnp.float32, jnp.bfloat16
    dma = pltpu.SemaphoreType.DMA
    return pl.pallas_call(
        functools.partial(fused_kernel, bands, owned, slots),
        out_shape=jax.ShapeDtypeStruct((owned, width), f32),
        in_specs=[vmem] * 5,
        out_specs=vmem,
        scratch_shapes=[
            pltpu.VMEM((bands, owned, width), f32),
            pltpu.VMEM((bands, owned, width), f32),
            pltpu.VMEM((bands, owned, width), f32),
            pltpu.VMEM((doms, owned + 8, size), f32),
            pltpu.VMEM((doms, size, 2 * size), b16),
            pltpu.VMEM((doms, 2 * slots, owned), b16),
            pltpu.VMEM((doms, owned, 2 * slots), b16),
            pltpu.VMEM((doms, rows, LANES), f32),
            pltpu.VMEM((doms, rows, LANES), f32),
            pltpu.VMEM((doms, 2 * size, LANES), b16),
            pltpu.VMEM((doms, 2 * slots, LANES), b16),
            pltpu.VMEM((doms, owned, LANES), f32),
            pltpu.VMEM((doms, owned, LANES), f32),
            pltpu.VMEM((doms, owned, LANES), f32),
            pltpu.VMEM((doms, rows, LANES), f32),
            pltpu.VMEM((doms, rows, LANES), f32),
            dma((bands, CUTS)), dma((bands, CUTS)), dma((bands, CUTS)),
            dma((7,)), dma((doms,)),
            dma((doms, CUTS)), dma((doms, CUTS)),
            dma((doms,)), dma((doms,)),
        ],
        compiler_params=pltpu.CompilerParams(
            vmem_limit_bytes=56 * 2**20, collective_id=0, has_side_effects=True),
        cost_estimate=pl.CostEstimate(
            flops=DEGREE * doms * 4 * size * size * LANES, bytes_accessed=2**24, transcendentals=0),
    )(waves, jnp.swapaxes(cell_matrix, 0, 1), connect, send_index, rotation)


def shards(waves, cell_matrix, connect, send_index, rotation):
    owned = waves.shape[0]
    width = waves.shape[1]
    slots = send_index.shape[2]
    doms = lax.axis_size("dom")
    if doms == 8 and width == doms * LANES // 2 and 2 * slots == LANES and owned == 2 * LANES and lax.axis_size("band") == 4:
        return fused(waves, cell_matrix, connect, send_index, rotation)
    size = owned + 2 * slots
    seat = jax.nn.one_hot(connect, size, dtype=jnp.float32)
    half_way = jnp.einsum("cij,cjn->cin", cell_matrix, seat, precision=lax.Precision.HIGH)
    local = jnp.einsum("cim,cin->mn", seat, half_way, precision=lax.Precision.HIGH)
    node = jnp.arange(size)
    shift = jnp.where((node[:, None] == node[None, :]) & (node[:, None] < owned), centre, 0.0)
    local = (local - shift) / half_width
    row = jnp.zeros((8, size), jnp.float32).at[0, : 2 * slots].set(
        send_index.reshape(-1).astype(jnp.float32)
    )
    everyone = lax.all_gather(jnp.concatenate([local, row], axis=0), "dom")
    high, low = split(everyone[:, :size])
    index = everyone[:, size, : 2 * slots].astype(jnp.int32)
    pick = jax.nn.one_hot(index, owned, dtype=jnp.bfloat16)
    spread = jnp.swapaxes(pick, 1, 2)

    partial = jnp.dot(waves, rotation, precision=lax.Precision.HIGH, preferred_element_type=jnp.float32)
    turned = lax.psum_scatter(partial, "band", scatter_dimension=1, tiled=True)
    share = width // doms
    columns = lax.all_to_all(turned, "dom", split_axis=1, concat_axis=0, tiled=True)
    columns = columns.reshape(doms, owned, share)
    half = LANES // 2
    columns = jnp.pad(columns, ((0, 0), (0, 0), (0, half - share)))
    columns = jnp.concatenate([columns, columns], axis=2)
    vmem = pl.BlockSpec(memory_space=pltpu.VMEM)
    done = pl.pallas_call(
        functools.partial(filter_kernel, doms, owned, slots, half),
        out_shape=jax.ShapeDtypeStruct((doms, owned, LANES), jnp.float32),
        in_specs=[vmem] * 5,
        out_specs=vmem,
        scratch_shapes=[
            pltpu.VMEM((doms, size, LANES), jnp.bfloat16),
            pltpu.VMEM((doms, 2 * slots, LANES), jnp.bfloat16),
            pltpu.VMEM((doms, owned, LANES), jnp.float32),
            pltpu.VMEM((doms, owned, LANES), jnp.float32),
        ],
        compiler_params=pltpu.CompilerParams(vmem_limit_bytes=56 * 2**20),
        cost_estimate=pl.CostEstimate(
            flops=DEGREE * doms * 4 * size * size * LANES, bytes_accessed=2**24, transcendentals=0
        ),
    )(high, low, pick, spread, columns)
    back = done[:, :, :share].reshape(doms * owned, share)
    return lax.all_to_all(back, "dom", split_axis=0, concat_axis=1, tiled=True)


def solution(mesh):
    in_specs = (
        P("dom", "band"),
        P("dom", None, None),
        P("dom", None),
        P("dom", None, None),
        P("band", None),
    )
    out_specs = P("dom", "band")
    return jax.shard_map(shards, mesh=mesh, in_specs=in_specs, out_specs=out_specs, check_vma=False)
```

profile of v0, /device:TPU:17, one launch (start us, length us, event | category | flops | bytes accessed | tf_op | source)
XLA Modules:
  0.0 80.6 jit_solution(2616603891614991092)
XLA Ops:
  0.0 78.7 %shard_map.55 = f32[256,512]{1,0:T(8,128)} custom-call(f32[256,512]{1,0:T(8,128)} %waves.1, f32[125,8,125]{2,1,0:T(8,128)} %bitcast.1, s32[8,125]{1,0:T(8,128)} %conn.1, s32[1,2,64]{2,1,0:T(2,128)} %send.1, f32[512,2048]{1,0:T(8,128)} %rotation.1), custom_call_target="tpu_custom_call" | custom-call | flops 4831838208 | bytes 16777216 | tf_op jit(solution)/shard_map/pallas_call | solution.py:415
  78.7 1.9 %copy.7 = f32[256,512]{1,0:T(8,128)} copy(f32[256,512]{1,0:T(8,128)} %shard_map.55) | data formatting | bytes 1048576
where the time goes:
time: 81.3 us; the launch traced here: 80.6 us
  Pallas kernels  78.7 us (97%)
  local copies, waits for them, and re-layouts  1.87 us (2%)
    pallas_call x1, Pallas kernels, fused(): pl.pallas_call(functools.partial(fused_kernel, bands, owned, slots), out_...  78.7 us
    unnamed x1, local copies, waits for them, and re-layouts  1.87 us

commit v1 on v0

v1 whole, which is shorter than its diff:
```python
import functools

import jax
import jax.numpy as jnp
from jax import lax
from jax.experimental import pallas as pl
from jax.experimental.pallas import tpu as pltpu
from jax.sharding import PartitionSpec as P

DEGREE = 8
LANES = 128
MESH = pl.DeviceIdType.MESH
CUTS = 4
ORDER = ((3, 0), (3, 1), (2, 0), (1, 0), (3, 2), (2, 1), (1, 1), (3, 3), (2, 2), (1, 2), (2, 3), (1, 3))


centre = 5.5
half_width = 9.5


def split(x):
    high = lax.reduce_precision(x, 8, 7)
    return high.astype(jnp.bfloat16), (x - high).astype(jnp.bfloat16)


def doubled(x, half):
    return x + pltpu.roll(x, half, 1)


def packed(x, half):
    high = x.astype(jnp.bfloat16)
    low = (x - high.astype(jnp.float32)).astype(jnp.bfloat16)
    lane = lax.broadcasted_iota(jnp.int32, x.shape, 1)
    return jnp.where(lane < half, high.astype(jnp.float32), low.astype(jnp.float32)).astype(
        jnp.bfloat16
    )


def mm(a, b):
    return jnp.dot(a, b, preferred_element_type=jnp.float32)


def filter_kernel(doms, owned, slots, half, high, low, pick, spread, start, out, pieces, ghosts, before, image):
    unroll = doms <= 8

    def over(body):
        if unroll:
            for d in range(doms):
                body(d)
        else:
            pl.loop(0, doms)(body)

    def begin(d):
        v = start[d]
        out[d] = v
        before[d] = jnp.zeros_like(v)
        pieces[d, :owned] = packed(v, half)

    over(begin)

    def one(step, _):
        def send(d):
            after = lax.rem(d + 1, doms) if not unroll else (d + 1) % doms
            ahead = lax.rem(d + doms - 1, doms) if not unroll else (d - 1) % doms
            g = mm(pick[d], pieces[d, :owned]).astype(jnp.bfloat16)
            pieces[after, owned : owned + slots] = g[:slots]
            pieces[ahead, owned + slots :] = g[slots:]

        over(send)

        def apply(d):
            x = pieces[d]
            y = mm(high[d], x) + mm(low[d], x)
            y = doubled(y, half)
            image[d] = y[:owned]
            after = lax.rem(d + 1, doms) if not unroll else (d + 1) % doms
            ahead = lax.rem(d + doms - 1, doms) if not unroll else (d - 1) % doms
            r = packed(y[owned:], half)
            ghosts[ahead, :slots] = r[:slots]
            ghosts[after, slots:] = r[slots:]

        over(apply)
        scale = jnp.where(step == 0, 1.0, 2.0)

        def update(d):
            y = image[d] + doubled(mm(spread[d], ghosts[d]), half)
            v = scale * y - before[d]
            before[d] = out[d]
            out[d] = v
            pieces[d, :owned] = packed(v, half)

        over(update)
        return 0

    lax.fori_loop(0, DEGREE, one, 0)


def high_low(x):
    high = x.astype(jnp.bfloat16)
    return high, (x - high.astype(jnp.float32)).astype(jnp.bfloat16)


def fused_kernel(bands, owned, slots, waves, cells, conn, send, rotation, out, *scratch):
    (acc, from_left, from_right, everyone, matrix, pick, spread, pieces, ghosts, image, even, odd,
     gathered, y_high, y_low, p_high, p_low,
     z_send, z_right, z_left, m_send, m_recv, y_send, y_recv) = scratch
    doms = 8
    size = owned + 2 * slots
    rows = owned // 2
    b16 = jnp.bfloat16
    me = lax.axis_index("dom")
    z = lax.axis_index("band")
    core = lax.rem(me, 2)
    place = lax.rem(lax.div(me, 2), 2)
    upper = lax.div(me, 4)
    sib = me + 1 - 2 * core
    x_next = me + 2 - 4 * place
    y_next = me + 4 - 8 * upper
    diag = x_next + 4 - 8 * upper
    across = x_next * (1 - core) + y_next * core
    onward = y_next * (1 - core) + x_next * core

    def seat_of(dom, at):
        return lax.rem(dom - at + doms, doms)

    barrier = pltpu.get_barrier_semaphore()
    for t in range(1, doms):
        pl.semaphore_signal(barrier, inc=1, device_id={"dom": lax.rem(me + t, doms)}, device_id_type=MESH)

    @pl.when(z > 0)
    def _():
        pl.semaphore_signal(barrier, inc=1, device_id={"band": z - 1}, device_id_type=MESH)

    @pl.when(z < bands - 1)
    def _():
        pl.semaphore_signal(barrier, inc=1, device_id={"band": z + 1}, device_id_type=MESH)

    beside = lax.div(z + bands - 1, bands) + lax.div(2 * bands - 2 - z, bands)
    pl.semaphore_wait(barrier, doms - 1 + beside)

    def to_right(j, c):
        return pltpu.make_async_remote_copy(
            src_ref=acc.at[j, c], dst_ref=from_left.at[j, c], send_sem=z_send.at[j, c],
            recv_sem=z_right.at[j, c], device_id={"band": z + 1}, device_id_type=MESH)

    def to_left(j, c):
        return pltpu.make_async_remote_copy(
            src_ref=acc.at[j, c], dst_ref=from_right.at[j, c], send_sem=z_send.at[j, c],
            recv_sem=z_left.at[j, c], device_id={"band": z - 1}, device_id_type=MESH)

    def send_right(items):
        @pl.when(z == 0)
        def _():
            for j, c in items:
                to_right(j, c).start()

    def send_left(items):
        @pl.when(z == bands - 1)
        def _():
            for j, c in items:
                to_left(bands - 1 - j, c).start()

    w_high, w_low = high_low(waves[...])
    width = waves.shape[1]

    def partial(j):
        r_high, r_low = high_low(rotation[:, j * width : (j + 1) * width])
        y = mm(w_high, r_high) + (mm(w_high, r_low) + mm(w_low, r_high))
        for c in range(CUTS):
            acc[j, c] = y[:, c * LANES : (c + 1) * LANES]

    partial(3)
    send_right(ORDER[:2])
    partial(0)
    send_left(ORDER[:2])

    node = lax.broadcasted_iota(jnp.int32, (size, conn.shape[1]), 0)
    total = jnp.zeros((size, size), jnp.float32)
    for c in range(cells.shape[1]):
        seat = jnp.where(node == conn[c : c + 1, :], 1.0, 0.0).astype(b16)
        a_high, a_low = high_low(cells[:, c, :])
        b_high, b_low = high_low(mm(seat, a_high) + mm(seat, a_low))
        dims = (((1,), (1,)), ((), ()))
        total = total + (
            lax.dot_general(b_high, seat, dims, preferred_element_type=jnp.float32)
            + lax.dot_general(b_low, seat, dims, preferred_element_type=jnp.float32))
    r_at = lax.broadcasted_iota(jnp.int32, (size, size), 0)
    c_at = lax.broadcasted_iota(jnp.int32, (size, size), 1)
    shift = jnp.where((r_at == c_at) & (r_at < owned), centre, 0.0)
    total = (total - shift) / half_width
    everyone[0, :rows] = total[:rows]
    everyone[0, rows:owned, rows:] = total[rows:owned, rows:]
    everyone[0, rows:owned, :rows] = total[owned:, owned:]
    everyone[0, owned:] = jnp.zeros((8, size), jnp.float32)
    everyone[0, owned : owned + 2, :slots] = send[0].astype(jnp.float32)

    def m_copy(dom, to, k):
        return pltpu.make_async_remote_copy(
            src_ref=everyone.at[seat_of(dom, me)], dst_ref=everyone.at[seat_of(dom, to)], send_sem=m_send.at[k],
            recv_sem=m_recv.at[seat_of(dom, to)], device_id={"dom": to}, device_id_type=MESH)

    def m_wait(dom):
        pltpu.make_async_remote_copy(
            src_ref=everyone.at[0], dst_ref=everyone.at[seat_of(dom, me)], send_sem=m_send.at[0],
            recv_sem=m_recv.at[seat_of(dom, me)], device_id={"dom": sib}, device_id_type=MESH).wait_recv()

    def y_copy(c, dom, to, k):
        return pltpu.make_async_remote_copy(
            src_ref=gathered.at[seat_of(dom, me), c], dst_ref=gathered.at[seat_of(dom, to), c],
            send_sem=y_send.at[c, k], recv_sem=y_recv.at[c, seat_of(dom, to)], device_id={"dom": to},
            device_id_type=MESH)

    def y_wait(c, dom):
        pltpu.make_async_remote_copy(
            src_ref=gathered.at[0, c], dst_ref=gathered.at[seat_of(dom, me), c], send_sem=y_send.at[c, 0],
            recv_sem=y_recv.at[c, seat_of(dom, me)], device_id={"dom": sib}, device_id_type=MESH).wait_recv()

    unsent = []

    def go(copy):
        copy.start()
        unsent.append(copy)

    def first_hop(copy):
        go(copy(me, x_next, 0))
        go(copy(me, y_next, 1))
        go(copy(me, sib, 2))

    def second_hop(copy, wait):
        wait(x_next)
        wait(y_next)
        go(copy(across, onward, 3))
        go(copy(x_next, sib, 4))
        go(copy(y_next, sib, 5))

    def third_hop(copy, wait):
        wait(diag)
        go(copy(diag, sib, 6))

    away = [sib, x_next + 1 - 2 * core, y_next + 1 - 2 * core, diag + 1 - 2 * core]

    first_hop(m_copy)

    partial(2)
    partial(1)
    send_right(ORDER[2:])
    send_left(ORDER[2:])

    def relay(k):
        def right(j, c):
            to_right(j, c).wait_recv()
            acc[j, c] = acc[j, c] + from_left[j, c]
            to_right(j, c).start()

        def left(j, c):
            to_left(j, c).wait_recv()
            acc[j, c] = acc[j, c] + from_right[j, c]
            to_left(j, c).start()

        last = bands - 1
        for hop in (1, 2):
            at = k - hop + 1
            if not 0 <= at < len(ORDER):
                continue
            j, c = ORDER[at]
            if j > hop:
                @pl.when(z == hop)
                def _():
                    right(j, c)

                @pl.when(z == last - hop)
                def _():
                    left(last - j, c)

    def finish(c):
        gathered[0, c] = acc[z, c]

        @pl.when(z > 0)
        def _():
            to_right(z, c).wait_recv()
            gathered[0, c] = gathered[0, c] + from_left[z, c]

        @pl.when(z < bands - 1)
        def _():
            to_left(z, c).wait_recv()
            gathered[0, c] = gathered[0, c] + from_right[z, c]

        first_hop(functools.partial(y_copy, c))

    def y_second(c):
        second_hop(functools.partial(y_copy, c), functools.partial(y_wait, c))

    def y_third(c):
        third_hop(functools.partial(y_copy, c), functools.partial(y_wait, c))

    def y_split(c):
        for dom in away:
            y_wait(c, dom)
        columns = slice(c * LANES, (c + 1) * LANES)
        for d in range(doms):
            high, low = high_low(gathered[d, c])
            y_high[d * owned : (d + 1) * owned, columns] = high
            y_low[d * owned : (d + 1) * owned, columns] = low

    def prepare(d):
        upper_rows = everyone[d, :rows]
        middle = everyone[d, rows:owned]
        whole = jnp.concatenate([
            upper_rows,
            jnp.concatenate([jnp.transpose(upper_rows[:, rows:owned]), middle[:, rows:]], axis=1),
            jnp.concatenate([
                jnp.transpose(upper_rows[:, owned:]), jnp.transpose(middle[:, owned:]),
                middle[:, :rows]], axis=1)], axis=0)
        m_high, m_low = high_low(whole)
        matrix[d, :, :size] = m_high
        matrix[d, :, size : 2 * size] = m_low
        matrix[d, :, 2 * size :] = m_high
        tile = everyone[d, owned:, :LANES]
        other = pltpu.roll(tile, slots, 1)
        first_lanes = lax.broadcasted_iota(jnp.int32, (1, LANES), 1) < slots
        row = jnp.where(first_lanes, tile[0:1], other[1:2]).astype(jnp.int32)
        at = lax.broadcasted_iota(jnp.int32, (owned, LANES), 0)
        hot = jnp.where(at == row, 1.0, 0.0)
        spread[d, :, :LANES] = hot.astype(b16)
        spread[d, :, LANES:] = hot.astype(b16)
        pick[d] = jnp.transpose(hot).astype(b16)

    pieces[...] = jnp.zeros_like(pieces)
    ghosts[...] = jnp.zeros_like(ghosts)
    i_at = lax.broadcasted_iota(jnp.int32, (owned, owned), 0)
    j_at = lax.broadcasted_iota(jnp.int32, (owned, owned), 1)
    eye = jnp.where(i_at == j_at, 1.0, 0.0)
    even[0] = eye
    pieces[0, :owned] = eye.astype(b16)
    pieces[0, size : size + owned] = eye.astype(b16)
    prepare(0)

    relay(0)
    relay(1)
    relay(2)
    second_hop(m_copy, m_wait)
    relay(3)
    finish(0)
    relay(4)
    third_hop(m_copy, m_wait)
    for dom in away:
        m_wait(dom)
    for d in range(1, doms):
        prepare(d)
    relay(5)

    every = list(range(doms))
    held = [[0], [6, 7, 0, 1, 2]]
    busy = [[7, 0, 1], [5, 6, 7, 0, 1, 2, 3]]

    def advance(k, end):
        source = held[k - 1] if k <= 2 else every
        active = busy[k - 1] if k <= 2 else every
        result = held[k] if k < 2 else every
        old = [] if k == 1 else held[k - 2] if k <= 3 else every
        store = odd if k % 2 else even
        for d in source:
            after, ahead = (d + 1) % doms, (d - 1) % doms
            for at, bases in ((0, (0, size)), (2 * size, (2 * size,))):
                g = mm(pick[d], pieces[d, at : at + owned]).astype(b16)
                for base in bases:
                    pieces[after, base + owned : base + owned + slots] = g[:slots]
                    pieces[ahead, base + owned + slots : base + size] = g[slots:]
        for d in active:
            after, ahead = (d + 1) % doms, (d - 1) % doms
            y = mm(matrix[d], pieces[d])
            image[d] = y[:owned]
            high, low = high_low(y[owned:])
            ghosts[ahead, :slots] = high[:slots]
            ghosts[ahead, 2 * slots : 3 * slots] = low[:slots]
            ghosts[after, slots : 2 * slots] = high[slots:]
            ghosts[after, 3 * slots :] = low[slots:]
        for d in result:
            y = mm(spread[d], ghosts[d])
            if d in active:
                y = y + image[d]
            v = y if k == 1 else 2.0 * y
            if d in old:
                v = v - store[d]
            if end:
                high, low = high_low(jnp.transpose(v))
                p_high[:, d * owned : (d + 1) * owned] = high
                p_low[:, d * owned : (d + 1) * owned] = low
            else:
                store[d] = v
                high, low = high_low(v)
                pieces[d, :owned] = high
                pieces[d, size : size + owned] = high
                pieces[d, 2 * size : 2 * size + owned] = low

    advance(1, False)
    y_second(0)
    relay(6)
    finish(1)
    advance(2, False)
    relay(7)
    y_third(0)
    advance(3, False)
    relay(8)
    y_second(1)
    y_split(0)
    advance(4, False)
    relay(9)
    finish(2)
    y_third(1)
    advance(5, False)
    relay(10)
    y_second(2)
    y_split(1)
    advance(6, False)
    relay(11)
    finish(3)
    y_third(2)
    advance(7, False)
    relay(12)
    y_second(3)
    y_split(2)
    advance(8, True)
    y_third(3)
    y_split(3)
    for h in range(width // owned):
        columns = slice(h * owned, (h + 1) * owned)
        high, low = y_high[:, columns], y_low[:, columns]
        out[:, columns] = mm(p_high[...], high) + (mm(p_high[...], low) + mm(p_low[...], high))

    for copy in unsent:
        copy.wait_send()
    for j in range(bands):
        for c in range(CUTS):
            @pl.when(z < j)
            def _():
                to_right(j, c).wait_send()

            @pl.when(z > j)
            def _():
                to_left(j, c).wait_send()


def fused(waves, cell_matrix, connect, send_index, rotation):
    owned, width = waves.shape
    slots = send_index.shape[2]
    bands = lax.axis_size("band")
    size = owned + 2 * slots
    doms = 8
    vmem = pl.BlockSpec(memory_space=pltpu.VMEM)
    f32, b16 = jnp.float32, jnp.bfloat16
    dma = pltpu.SemaphoreType.DMA
    return pl.pallas_call(
        functools.partial(fused_kernel, bands, owned, slots),
        out_shape=jax.ShapeDtypeStruct((owned, width), f32),
        in_specs=[vmem] * 5,
        out_specs=vmem,
        scratch_shapes=[
            pltpu.VMEM((bands, CUTS, owned, LANES), f32),
            pltpu.VMEM((bands, CUTS, owned, LANES), f32),
            pltpu.VMEM((bands, CUTS, owned, LANES), f32),
            pltpu.VMEM((doms, owned + 8, size), f32),
            pltpu.VMEM((doms, size, 3 * size), b16),
            pltpu.VMEM((doms, 2 * slots, owned), b16),
            pltpu.VMEM((doms, owned, 4 * slots), b16),
            pltpu.VMEM((doms, 3 * size, owned), b16),
            pltpu.VMEM((doms, 4 * slots, owned), b16),
            pltpu.VMEM((doms, owned, owned), f32),
            pltpu.VMEM((doms, owned, owned), f32),
            pltpu.VMEM((doms, owned, owned), f32),
            pltpu.VMEM((doms, CUTS, owned, LANES), f32),
            pltpu.VMEM((doms * owned, width), b16),
            pltpu.VMEM((doms * owned, width), b16),
            pltpu.VMEM((owned, doms * owned), b16),
            pltpu.VMEM((owned, doms * owned), b16),
            dma((bands, CUTS)), dma((bands, CUTS)), dma((bands, CUTS)),
            dma((7,)), dma((doms,)),
            dma((CUTS, 7)), dma((CUTS, doms)),
        ],
        compiler_params=pltpu.CompilerParams(
            vmem_limit_bytes=60 * 2**20, collective_id=0, has_side_effects=True),
        cost_estimate=pl.CostEstimate(
            flops=DEGREE * doms * 6 * size * size * owned, bytes_accessed=2**24, transcendentals=0),
    )(waves, jnp.swapaxes(cell_matrix, 0, 1), connect, send_index, rotation)


def shards(waves, cell_matrix, connect, send_index, rotation):
    owned = waves.shape[0]
    width = waves.shape[1]
    slots = send_index.shape[2]
    doms = lax.axis_size("dom")
    if doms == 8 and width == doms * LANES // 2 and 2 * slots == LANES and owned == 2 * LANES and lax.axis_size("band") == 4:
        return fused(waves, cell_matrix, connect, send_index, rotation)
    size = owned + 2 * slots
    seat = jax.nn.one_hot(connect, size, dtype=jnp.float32)
    half_way = jnp.einsum("cij,cjn->cin", cell_matrix, seat, precision=lax.Precision.HIGH)
    local = jnp.einsum("cim,cin->mn", seat, half_way, precision=lax.Precision.HIGH)
    node = jnp.arange(size)
    shift = jnp.where((node[:, None] == node[None, :]) & (node[:, None] < owned), centre, 0.0)
    local = (local - shift) / half_width
    row = jnp.zeros((8, size), jnp.float32).at[0, : 2 * slots].set(
        send_index.reshape(-1).astype(jnp.float32)
    )
    everyone = lax.all_gather(jnp.concatenate([local, row], axis=0), "dom")
    high, low = split(everyone[:, :size])
    index = everyone[:, size, : 2 * slots].astype(jnp.int32)
    pick = jax.nn.one_hot(index, owned, dtype=jnp.bfloat16)
    spread = jnp.swapaxes(pick, 1, 2)

    partial = jnp.dot(waves, rotation, precision=lax.Precision.HIGH, preferred_element_type=jnp.float32)
    turned = lax.psum_scatter(partial, "band", scatter_dimension=1, tiled=True)
    share = width // doms
    columns = lax.all_to_all(turned, "dom", split_axis=1, concat_axis=0, tiled=True)
    columns = columns.reshape(doms, owned, share)
    half = LANES // 2
    columns = jnp.pad(columns, ((0, 0), (0, 0), (0, half - share)))
    columns = jnp.concatenate([columns, columns], axis=2)
    vmem = pl.BlockSpec(memory_space=pltpu.VMEM)
    done = pl.pallas_call(
        functools.partial(filter_kernel, doms, owned, slots, half),
        out_shape=jax.ShapeDtypeStruct((doms, owned, LANES), jnp.float32),
        in_specs=[vmem] * 5,
        out_specs=vmem,
        scratch_shapes=[
            pltpu.VMEM((doms, size, LANES), jnp.bfloat16),
            pltpu.VMEM((doms, 2 * slots, LANES), jnp.bfloat16),
            pltpu.VMEM((doms, owned, LANES), jnp.float32),
            pltpu.VMEM((doms, owned, LANES), jnp.float32),
        ],
        compiler_params=pltpu.CompilerParams(vmem_limit_bytes=56 * 2**20),
        cost_estimate=pl.CostEstimate(
            flops=DEGREE * doms * 4 * size * size * LANES, bytes_accessed=2**24, transcendentals=0
        ),
    )(high, low, pick, spread, columns)
    back = done[:, :, :share].reshape(doms * owned, share)
    return lax.all_to_all(back, "dom", split_axis=0, concat_axis=1, tiled=True)


def solution(mesh):
    in_specs = (
        P("dom", "band"),
        P("dom", None, None),
        P("dom", None),
        P("dom", None, None),
        P("band", None),
    )
    out_specs = P("dom", "band")
    return jax.shard_map(shards, mesh=mesh, in_specs=in_specs, out_specs=out_specs, check_vma=False)
```

time: 81.3 us -> 69.3 us (0.85)
  Pallas kernels: 78.7 us -> 67.1 us
    pallas_call x1, Pallas kernels: 78.7 us -> 67.1 us  [fused(): pl.pallas_call(functools.partial(fused_kernel, bands, owned, slots), out_...]
where the time goes in v1:
time: 69.3 us; the launch traced here: 69 us
  Pallas kernels  67.1 us (97%)
  local copies, waits for them, and re-layouts  1.87 us (3%)
    pallas_call x1, Pallas kernels, fused(): pl.pallas_call(functools.partial(fused_kernel, bands, owned, slots), out_...  67.1 us
    unnamed x1, local copies, waits for them, and re-layouts  1.87 us

profile of v1, /device:TPU:17, one launch (start us, length us, event | category | flops | bytes accessed | tf_op | source)
XLA Modules:
  0.0 69.0 jit_solution(15848722403632704262)
XLA Ops:
  0.0 67.1 %shard_map.55 = f32[256,512]{1,0:T(8,128)} custom-call(f32[256,512]{1,0:T(8,128)} %waves.1, f32[125,8,125]{2,1,0:T(8,128)} %bitcast.1, s32[8,125]{1,0:T(8,128)} %conn.1, s32[1,2,64]{2,1,0:T(2,128)} %send.1, f32[512,2048]{1,0:T(8,128)} %rotation.1), custom_call_target="tpu_custom_call" | custom-call | flops 14495514624 | bytes 16777216 | tf_op jit(solution)/shard_map/pallas_call | solution.py:453
  67.1 1.9 %copy.7 = f32[256,512]{1,0:T(8,128)} copy(f32[256,512]{1,0:T(8,128)} %shard_map.55) | data formatting | bytes 1048576

commit v2 on v1

--- a/solution.py
+++ b/solution.py
@@ -10,8 +10,10 @@
 DEGREE = 8
 LANES = 128
 MESH = pl.DeviceIdType.MESH
-CUTS = 4
-ORDER = ((3, 0), (3, 1), (2, 0), (1, 0), (3, 2), (2, 1), (1, 1), (3, 3), (2, 2), (1, 2), (2, 3), (1, 3))
+SPAN = ((0, 64), (64, 64), (128, 64), (192, 32), (224, 32))
+ORDER = ((3, 0), (3, 1), (2, 0), (1, 0), (3, 2), (2, 1), (1, 1), (3, 3), (2, 2), (1, 2), (3, 4), (2, 3), (2, 4),
+         (1, 3), (1, 4))
+HALVES = ((0, 104), (104, 96))
 
 
 centre = 5.5
@@ -100,8 +102,8 @@
     return high, (x - high.astype(jnp.float32)).astype(jnp.bfloat16)
 
 
-def fused_kernel(bands, owned, slots, waves, cells, conn, send, rotation, out, *scratch):
-    (acc, from_left, from_right, everyone, matrix, pick, spread, pieces, ghosts, image, even, odd,
+def fused_kernel(bands, owned, slots, waves_in, cells_in, conn, send, rotation_in, out, *scratch):
+    (waves, cells, rotation, load, acc, from_left, from_right, everyone, matrix, pick, spread, pieces, ghosts, image, even, odd,
      gathered, y_high, y_low, p_high, p_low,
      z_send, z_right, z_left, m_send, m_recv, y_send, y_recv) = scratch
     doms = 8
@@ -135,17 +137,31 @@
     def _():
         pl.semaphore_signal(barrier, inc=1, device_id={"band": z + 1}, device_id_type=MESH)
 
-    beside = lax.div(z + bands - 1, bands) + lax.div(2 * bands - 2 - z, bands)
-    pl.semaphore_wait(barrier, doms - 1 + beside)
+    width = waves.shape[1]
+
+    def block(j):
+        return pl.ds(j * width, width)
+
+    order = []
+    for r in range(bands // 2):
+        order += [bands - 1 - r, r]
+    loads = [pltpu.make_async_copy(waves_in, waves, load.at[bands + 1])]
+    loads += [pltpu.make_async_copy(rotation_in.at[:, block(j)], rotation.at[:, block(j)], load.at[j]) for j in order]
+    loads.insert(3, pltpu.make_async_copy(cells_in, cells, load.at[bands]))
+    for copy in loads:
+        copy.start()
+
+    def rows_of(c):
+        return pl.ds(*SPAN[c])
 
     def to_right(j, c):
         return pltpu.make_async_remote_copy(
-            src_ref=acc.at[j, c], dst_ref=from_left.at[j, c], send_sem=z_send.at[j, c],
+            src_ref=acc.at[j, rows_of(c)], dst_ref=from_left.at[j, rows_of(c)], send_sem=z_send.at[j, c],
             recv_sem=z_right.at[j, c], device_id={"band": z + 1}, device_id_type=MESH)
 
     def to_left(j, c):
         return pltpu.make_async_remote_copy(
-            src_ref=acc.at[j, c], dst_ref=from_right.at[j, c], send_sem=z_send.at[j, c],
+            src_ref=acc.at[j, rows_of(c)], dst_ref=from_right.at[j, rows_of(c)], send_sem=z_send.at[j, c],
             recv_sem=z_left.at[j, c], device_id={"band": z - 1}, device_id_type=MESH)
 
     def send_right(items):
@@ -160,20 +176,24 @@
             for j, c in items:
                 to_left(bands - 1 - j, c).start()
 
+    loads[0].wait()
     w_high, w_low = high_low(waves[...])
-    width = waves.shape[1]
 
     def partial(j):
         r_high, r_low = high_low(rotation[:, j * width : (j + 1) * width])
-        y = mm(w_high, r_high) + (mm(w_high, r_low) + mm(w_low, r_high))
-        for c in range(CUTS):
-            acc[j, c] = y[:, c * LANES : (c + 1) * LANES]
-
+        acc[j] = mm(w_high, r_high) + (mm(w_high, r_low) + mm(w_low, r_high))
+
+    loads[1].wait()
     partial(3)
+    loads[2].wait()
+    partial(0)
+    beside = lax.div(z + bands - 1, bands) + lax.div(2 * bands - 2 - z, bands)
+    pl.semaphore_wait(barrier, doms - 1 + beside)
+
     send_right(ORDER[:2])
-    partial(0)
     send_left(ORDER[:2])
 
+    loads[3].wait()
     node = lax.broadcasted_iota(jnp.int32, (size, conn.shape[1]), 0)
     total = jnp.zeros((size, size), jnp.float32)
     for c in range(cells.shape[1]):
@@ -188,32 +208,49 @@
     c_at = lax.broadcasted_iota(jnp.int32, (size, size), 1)
     shift = jnp.where((r_at == c_at) & (r_at < owned), centre, 0.0)
     total = (total - shift) / half_width
-    everyone[0, :rows] = total[:rows]
-    everyone[0, rows:owned, rows:] = total[rows:owned, rows:]
-    everyone[0, rows:owned, :rows] = total[owned:, owned:]
-    everyone[0, owned:] = jnp.zeros((8, size), jnp.float32)
-    everyone[0, owned : owned + 2, :slots] = send[0].astype(jnp.float32)
-
-    def m_copy(dom, to, k):
+    i_at = lax.broadcasted_iota(jnp.int32, (rows, rows), 0)
+    j_at = lax.broadcasted_iota(jnp.int32, (rows, rows), 1)
+    quarter = rows // 2
+    one, two, three = slice(0, rows), slice(rows, 2 * rows), slice(2 * rows, 3 * rows)
+    base, tail = slice(rows, rows + quarter), rows + quarter
+    corner = total[three, three]
+    top, bottom = corner[:quarter], pltpu.roll(corner[quarter:], quarter, 1)
+    mixed = jnp.where(i_at <= j_at, total[one, one], total[two, two])
+    everyone[0, one, one] = total[one, two]
+    everyone[0, one, two] = total[one, three]
+    everyone[0, one, three] = total[two, three]
+    everyone[0, base, one] = mixed[:quarter]
+    everyone[0, base, two] = mixed[quarter:]
+    everyone[0, base, three] = jnp.where((i_at <= j_at)[:quarter], top, bottom)
+    everyone[0, tail:] = jnp.zeros((8, size), jnp.float32)
+    everyone[0, tail : tail + 2, :slots] = send[0].astype(jnp.float32)
+    everyone[0, tail : tail + 1, two] = jnp.sum(
+        jnp.where(i_at == j_at, total[two, two], 0.0), axis=0, keepdims=True)
+    everyone[0, tail : tail + 1, three] = jnp.sum(jnp.where(i_at == j_at, corner, 0.0), axis=0, keepdims=True)
+
+    def m_copy(h, dom, to, k):
         return pltpu.make_async_remote_copy(
-            src_ref=everyone.at[seat_of(dom, me)], dst_ref=everyone.at[seat_of(dom, to)], send_sem=m_send.at[k],
-            recv_sem=m_recv.at[seat_of(dom, to)], device_id={"dom": to}, device_id_type=MESH)
-
-    def m_wait(dom):
+            src_ref=everyone.at[seat_of(dom, me), pl.ds(*HALVES[h])],
+            dst_ref=everyone.at[seat_of(dom, to), pl.ds(*HALVES[h])], send_sem=m_send.at[h, k],
+            recv_sem=m_recv.at[h, seat_of(dom, to)], device_id={"dom": to}, device_id_type=MESH)
+
+    def m_wait(h, dom):
+        part = everyone.at[seat_of(dom, me), pl.ds(*HALVES[h])]
         pltpu.make_async_remote_copy(
-            src_ref=everyone.at[0], dst_ref=everyone.at[seat_of(dom, me)], send_sem=m_send.at[0],
-            recv_sem=m_recv.at[seat_of(dom, me)], device_id={"dom": sib}, device_id_type=MESH).wait_recv()
+            src_ref=part, dst_ref=part, send_sem=m_send.at[h, 0], recv_sem=m_recv.at[h, seat_of(dom, me)],
+            device_id={"dom": sib}, device_id_type=MESH).wait_recv()
 
     def y_copy(c, dom, to, k):
         return pltpu.make_async_remote_copy(
-            src_ref=gathered.at[seat_of(dom, me), c], dst_ref=gathered.at[seat_of(dom, to), c],
+            src_ref=gathered.at[seat_of(dom, me), rows_of(c)], dst_ref=gathered.at[seat_of(dom, to), rows_of(c)],
             send_sem=y_send.at[c, k], recv_sem=y_recv.at[c, seat_of(dom, to)], device_id={"dom": to},
             device_id_type=MESH)
 
     def y_wait(c, dom):
+        part = gathered.at[seat_of(dom, me), rows_of(c)]
         pltpu.make_async_remote_copy(
-            src_ref=gathered.at[0, c], dst_ref=gathered.at[seat_of(dom, me), c], send_sem=y_send.at[c, 0],
-            recv_sem=y_recv.at[c, seat_of(dom, me)], device_id={"dom": sib}, device_id_type=MESH).wait_recv()
+            src_ref=part, dst_ref=part, send_sem=y_send.at[c, 0], recv_sem=y_recv.at[c, seat_of(dom, me)],
+            device_id={"dom": sib}, device_id_type=MESH).wait_recv()
 
     unsent = []
 
@@ -239,8 +276,13 @@
 
     away = [sib, x_next + 1 - 2 * core, y_next + 1 - 2 * core, diag + 1 - 2 * core]
 
-    first_hop(m_copy)
-
+    copies = [functools.partial(m_copy, h) for h in range(2)]
+    waits = [functools.partial(m_wait, h) for h in range(2)]
+    for h in range(2):
+        first_hop(copies[h])
+
+    for copy in loads[4:]:
+        copy.wait()
     partial(2)
     partial(1)
     send_right(ORDER[2:])
@@ -249,12 +291,12 @@
     def relay(k):
         def right(j, c):
             to_right(j, c).wait_recv()
-            acc[j, c] = acc[j, c] + from_left[j, c]
+            acc[j, rows_of(c)] = acc[j, rows_of(c)] + from_left[j, rows_of(c)]
             to_right(j, c).start()
 
         def left(j, c):
             to_left(j, c).wait_recv()
-            acc[j, c] = acc[j, c] + from_right[j, c]
+            acc[j, rows_of(c)] = acc[j, rows_of(c)] + from_right[j, rows_of(c)]
             to_left(j, c).start()
 
         last = bands - 1
@@ -273,17 +315,18 @@
                     left(last - j, c)
 
     def finish(c):
-        gathered[0, c] = acc[z, c]
+        part = rows_of(c)
+        gathered[0, part] = acc[z, part]
 
         @pl.when(z > 0)
         def _():
             to_right(z, c).wait_recv()
-            gathered[0, c] = gathered[0, c] + from_left[z, c]
+            gathered[0, part] = gathered[0, part] + from_left[z, part]
 
         @pl.when(z < bands - 1)
         def _():
             to_left(z, c).wait_recv()
-            gathered[0, c] = gathered[0, c] + from_right[z, c]
+            gathered[0, part] = gathered[0, part] + from_right[z, part]
 
         first_hop(functools.partial(y_copy, c))
 
@@ -296,26 +339,37 @@
     def y_split(c):
         for dom in away:
             y_wait(c, dom)
-        columns = slice(c * LANES, (c + 1) * LANES)
+        first, count = SPAN[c]
         for d in range(doms):
-            high, low = high_low(gathered[d, c])
-            y_high[d * owned : (d + 1) * owned, columns] = high
-            y_low[d * owned : (d + 1) * owned, columns] = low
+            high, low = high_low(gathered[d, first : first + count])
+            at = doms * first + d * count
+            y_high[at : at + count] = high
+            y_low[at : at + count] = low
 
     def prepare(d):
-        upper_rows = everyone[d, :rows]
-        middle = everyone[d, rows:owned]
-        whole = jnp.concatenate([
-            upper_rows,
-            jnp.concatenate([jnp.transpose(upper_rows[:, rows:owned]), middle[:, rows:]], axis=1),
-            jnp.concatenate([
-                jnp.transpose(upper_rows[:, owned:]), jnp.transpose(middle[:, owned:]),
-                middle[:, :rows]], axis=1)], axis=0)
-        m_high, m_low = high_low(whole)
-        matrix[d, :, :size] = m_high
-        matrix[d, :, size : 2 * size] = m_low
-        matrix[d, :, 2 * size :] = m_high
-        tile = everyone[d, owned:, :LANES]
+        straight = jnp.concatenate([everyone[d, base, one], everyone[d, base, two]], axis=0)
+        across_it = jnp.transpose(straight)
+        piece = everyone[d, base, three]
+        folded = jnp.concatenate([piece, pltpu.roll(piece, quarter, 1)], axis=0)
+        unfolded = jnp.transpose(folded)
+        second_line, third_line = everyone[d, tail : tail + 1, two], everyone[d, tail : tail + 1, three]
+        first_block = jnp.where(i_at <= j_at, straight, across_it)
+        second_block = jnp.where(i_at > j_at, straight, jnp.where(i_at < j_at, across_it, second_line))
+        direct = ((i_at < quarter) & (i_at <= j_at)) | ((j_at >= quarter) & (i_at > j_at))
+        third_block = jnp.where(
+            direct, folded, jnp.where((i_at == j_at) & (i_at >= quarter), third_line, unfolded))
+        ab, ac, bc = everyone[d, one, one], everyone[d, one, two], everyone[d, one, three]
+        lines = (
+            (one, (first_block, ab, ac)),
+            (two, (jnp.transpose(ab), second_block, bc)),
+            (three, (jnp.transpose(ac), jnp.transpose(bc), third_block)),
+        )
+        for line, blocks in lines:
+            m_high, m_low = high_low(jnp.concatenate(blocks, axis=1))
+            matrix[d, line, :size] = m_high
+            matrix[d, line, size : 2 * size] = m_low
+            matrix[d, line, 2 * size :] = m_high
+        tile = everyone[d, tail:, :LANES]
         other = pltpu.roll(tile, slots, 1)
         first_lanes = lax.broadcasted_iota(jnp.int32, (1, LANES), 1) < slots
         row = jnp.where(first_lanes, tile[0:1], other[1:2]).astype(jnp.int32)
@@ -327,33 +381,46 @@
 
     pieces[...] = jnp.zeros_like(pieces)
     ghosts[...] = jnp.zeros_like(ghosts)
-    i_at = lax.broadcasted_iota(jnp.int32, (owned, owned), 0)
-    j_at = lax.broadcasted_iota(jnp.int32, (owned, owned), 1)
-    eye = jnp.where(i_at == j_at, 1.0, 0.0)
+    eye = jnp.where(
+        lax.broadcasted_iota(jnp.int32, (owned, owned), 0) == lax.broadcasted_iota(jnp.int32, (owned, owned), 1),
+        1.0, 0.0)
     even[0] = eye
     pieces[0, :owned] = eye.astype(b16)
     pieces[0, size : size + owned] = eye.astype(b16)
     prepare(0)
 
+    def ready(dom):
+        prepare(seat_of(dom, me))
+
+    for wait in waits:
+        wait(sib)
+    ready(sib)
     relay(0)
+    second_hop(copies[0], waits[0])
     relay(1)
+    second_hop(copies[1], waits[1])
+    ready(x_next)
+    ready(y_next)
+    third_hop(copies[0], waits[0])
     relay(2)
-    second_hop(m_copy, m_wait)
+    for dom in away[1:3]:
+        for wait in waits:
+            wait(dom)
+        ready(dom)
+    third_hop(copies[1], waits[1])
+    ready(diag)
     relay(3)
+    for wait in waits:
+        wait(away[3])
+    ready(away[3])
     finish(0)
-    relay(4)
-    third_hop(m_copy, m_wait)
-    for dom in away:
-        m_wait(dom)
-    for d in range(1, doms):
-        prepare(d)
-    relay(5)
 
     every = list(range(doms))
     held = [[0], [6, 7, 0, 1, 2]]
     busy = [[7, 0, 1], [5, 6, 7, 0, 1, 2, 3]]
 
-    def advance(k, end):
+    def advance(k, middle=()):
+        end = k == DEGREE
         source = held[k - 1] if k <= 2 else every
         active = busy[k - 1] if k <= 2 else every
         result = held[k] if k < 2 else every
@@ -375,6 +442,8 @@
             ghosts[ahead, 2 * slots : 3 * slots] = low[:slots]
             ghosts[after, slots : 2 * slots] = high[slots:]
             ghosts[after, 3 * slots :] = low[slots:]
+        for act, c in middle:
+            act(c)
         for d in result:
             y = mm(spread[d], ghosts[d])
             if d in active:
@@ -383,9 +452,9 @@
             if d in old:
                 v = v - store[d]
             if end:
-                high, low = high_low(jnp.transpose(v))
-                p_high[:, d * owned : (d + 1) * owned] = high
-                p_low[:, d * owned : (d + 1) * owned] = low
+                for first, count in SPAN:
+                    at = doms * first + d * count
+                    odd[at // owned, at % owned : at % owned + count] = v[first : first + count]
             else:
                 store[d] = v
                 high, low = high_low(v)
@@ -393,45 +462,50 @@
                 pieces[d, size : size + owned] = high
                 pieces[d, 2 * size : 2 * size + owned] = low
 
-    advance(1, False)
+    advance(1)
+    advance(2, [(relay, 4)])
     y_second(0)
-    relay(6)
+    advance(3, [(relay, 5)])
+    y_third(0)
+    advance(4, [(relay, 6)])
+    relay(7)
     finish(1)
-    advance(2, False)
-    relay(7)
-    y_third(0)
-    advance(3, False)
-    relay(8)
-    y_second(1)
+    advance(5, [(relay, 8)])
     y_split(0)
-    advance(4, False)
-    relay(9)
+    advance(6, [(relay, 9), (y_second, 1)])
+    relay(10)
     finish(2)
-    y_third(1)
-    advance(5, False)
-    relay(10)
-    y_second(2)
+    advance(7, [(relay, 11), (y_third, 1)])
+    relay(12)
+    advance(8, [(y_second, 2), (relay, 13), (finish, 3)])
+    relay(14)
+    finish(4)
+    y_third(2)
     y_split(1)
-    advance(6, False)
-    relay(11)
-    finish(3)
-    y_third(2)
-    advance(7, False)
-    relay(12)
     y_second(3)
+    for d in range(doms):
+        high, low = high_low(jnp.transpose(odd[d]))
+        p_high[:, d * owned : (d + 1) * owned] = high
+        p_low[:, d * owned : (d + 1) * owned] = low
+    y_second(4)
     y_split(2)
-    advance(8, True)
     y_third(3)
+    y_third(4)
     y_split(3)
-    for h in range(width // owned):
-        columns = slice(h * owned, (h + 1) * owned)
-        high, low = y_high[:, columns], y_low[:, columns]
-        out[:, columns] = mm(p_high[...], high) + (mm(p_high[...], low) + mm(p_low[...], high))
+
+    def product(at):
+        high, low = y_high[at], y_low[at]
+        return mm(p_high[:, at], high) + (mm(p_high[:, at], low) + mm(p_low[:, at], high))
+
+    bulk = doms * SPAN[-1][0]
+    out[...] = product(slice(0, bulk))
+    y_split(4)
+    out[...] = out[...] + product(slice(bulk, doms * owned))
 
     for copy in unsent:
         copy.wait_send()
     for j in range(bands):
-        for c in range(CUTS):
+        for c in range(len(SPAN)):
             @pl.when(z < j)
             def _():
                 to_right(j, c).wait_send()
@@ -448,18 +522,24 @@
     size = owned + 2 * slots
     doms = 8
     vmem = pl.BlockSpec(memory_space=pltpu.VMEM)
+    anywhere = pl.BlockSpec(memory_space=pl.ANY)
+    cells = jnp.swapaxes(cell_matrix, 0, 1)
     f32, b16 = jnp.float32, jnp.bfloat16
     dma = pltpu.SemaphoreType.DMA
     return pl.pallas_call(
         functools.partial(fused_kernel, bands, owned, slots),
         out_shape=jax.ShapeDtypeStruct((owned, width), f32),
-        in_specs=[vmem] * 5,
+        in_specs=[anywhere, anywhere, vmem, vmem, anywhere],
         out_specs=vmem,
         scratch_shapes=[
-            pltpu.VMEM((bands, CUTS, owned, LANES), f32),
-            pltpu.VMEM((bands, CUTS, owned, LANES), f32),
-            pltpu.VMEM((bands, CUTS, owned, LANES), f32),
-            pltpu.VMEM((doms, owned + 8, size), f32),
+            pltpu.VMEM((owned, width), f32),
+            pltpu.VMEM(cells.shape, f32),
+            pltpu.VMEM(rotation.shape, f32),
+            dma((bands + 2,)),
+            pltpu.VMEM((bands, owned, width), f32),
+            pltpu.VMEM((bands, owned, width), f32),
+            pltpu.VMEM((bands, owned, width), f32),
+            pltpu.VMEM((doms, HALVES[1][0] + HALVES[1][1], size), f32),
             pltpu.VMEM((doms, size, 3 * size), b16),
             pltpu.VMEM((doms, 2 * slots, owned), b16),
             pltpu.VMEM((doms, owned, 4 * slots), b16),
@@ -468,20 +548,20 @@
             pltpu.VMEM((doms, owned, owned), f32),
             pltpu.VMEM((doms, owned, owned), f32),
             pltpu.VMEM((doms, owned, owned), f32),
-            pltpu.VMEM((doms, CUTS, owned, LANES), f32),
+            pltpu.VMEM((doms, owned, width), f32),
             pltpu.VMEM((doms * owned, width), b16),
             pltpu.VMEM((doms * owned, width), b16),
             pltpu.VMEM((owned, doms * owned), b16),
             pltpu.VMEM((owned, doms * owned), b16),
-            dma((bands, CUTS)), dma((bands, CUTS)), dma((bands, CUTS)),
-            dma((7,)), dma((doms,)),
-            dma((CUTS, 7)), dma((CUTS, doms)),
+            dma((bands, len(SPAN))), dma((bands, len(SPAN))), dma((bands, len(SPAN))),
+            dma((2, 7)), dma((2, doms)),
+            dma((len(SPAN), 7)), dma((len(SPAN), doms)),
         ],
         compiler_params=pltpu.CompilerParams(
             vmem_limit_bytes=60 * 2**20, collective_id=0, has_side_effects=True),
         cost_estimate=pl.CostEstimate(
             flops=DEGREE * doms * 6 * size * size * owned, bytes_accessed=2**24, transcendentals=0),
-    )(waves, jnp.swapaxes(cell_matrix, 0, 1), connect, send_index, rotation)
+    )(waves, cells, connect, send_index, rotation)
 
 
 def shards(waves, cell_matrix, connect, send_index, rotation):

time: 69.3 us -> 64.6 us (0.932)
  Pallas kernels: 67.1 us -> 62.1 us
    pallas_call x1, Pallas kernels: 67.1 us -> 62.1 us  [fused(): pl.pallas_call(functools.partial(fused_kernel, bands, owned, slots), out_...]
where the time goes in v2:
time: 64.6 us; the launch traced here: 63.9 us
  Pallas kernels  62.1 us (96%)
  local copies, waits for them, and re-layouts  1.87 us (3%)
    pallas_call x1, Pallas kernels, fused(): pl.pallas_call(functools.partial(fused_kernel, bands, owned, slots), out_...  62.1 us
    unnamed x1, local copies, waits for them, and re-layouts  1.87 us

profile of v2, /device:TPU:17, one launch (start us, length us, event | category | flops | bytes accessed | tf_op | source)
XLA Modules:
  0.0 63.9 jit_solution(15452568611362082447)
XLA Ops:
  0.0 62.1 %shard_map.55 = f32[256,512]{1,0:T(8,128)} custom-call(f32[256,512]{1,0:T(8,128)} %waves_in.1, f32[125,8,125]{2,1,0:T(8,128)} %bitcast.1, s32[8,125]{1,0:T(8,128)} %conn.1, s32[1,2,64]{2,1,0:T(2,128)} %send.1, f32[512,2048]{1,0:T(8,128)} %rotation_in.1), custom_call_target="tpu_custom_call" | custom-call | flops 14495514624 | bytes 16777216 | tf_op jit(solution)/shard_map/pallas_call | solution.py:529
  62.1 1.9 %copy.7 = f32[256,512]{1,0:T(8,128)} copy(f32[256,512]{1,0:T(8,128)} %shard_map.55) | data formatting | bytes 1048576

commit v3 on v2

--- a/solution.py
+++ b/solution.py
@@ -10,9 +10,11 @@
 DEGREE = 8
 LANES = 128
 MESH = pl.DeviceIdType.MESH
-SPAN = ((0, 64), (64, 64), (128, 64), (192, 32), (224, 32))
-ORDER = ((3, 0), (3, 1), (2, 0), (1, 0), (3, 2), (2, 1), (1, 1), (3, 3), (2, 2), (1, 2), (3, 4), (2, 3), (2, 4),
+SPAN = ((0, 96), (96, 64), (160, 48), (208, 32), (240, 16))
+ORDER = ((3, 0), (2, 0), (3, 1), (1, 0), (3, 2), (2, 1), (1, 1), (3, 3), (2, 2), (1, 2), (3, 4), (2, 3), (2, 4),
          (1, 3), (1, 4))
+FIRST, LINK, HOP, STOP, READY = 4.2, 2.8 / 64, 1.7, 0.2, 22.0
+STOPS = (3, 7)
 HALVES = ((0, 104), (104, 96))
 
 
@@ -190,8 +192,8 @@
     beside = lax.div(z + bands - 1, bands) + lax.div(2 * bands - 2 - z, bands)
     pl.semaphore_wait(barrier, doms - 1 + beside)
 
-    send_right(ORDER[:2])
-    send_left(ORDER[:2])
+    send_right(ORDER[:1])
+    send_left(ORDER[:1])
 
     loads[3].wait()
     node = lax.broadcasted_iota(jnp.int32, (size, conn.shape[1]), 0)
@@ -285,10 +287,10 @@
         copy.wait()
     partial(2)
     partial(1)
-    send_right(ORDER[2:])
-    send_left(ORDER[2:])
-
-    def relay(k):
+    send_right(ORDER[1:])
+    send_left(ORDER[1:])
+
+    def relay(k, hop):
         def right(j, c):
             to_right(j, c).wait_recv()
             acc[j, rows_of(c)] = acc[j, rows_of(c)] + from_left[j, rows_of(c)]
@@ -300,19 +302,15 @@
             to_left(j, c).start()
 
         last = bands - 1
-        for hop in (1, 2):
-            at = k - hop + 1
-            if not 0 <= at < len(ORDER):
-                continue
-            j, c = ORDER[at]
-            if j > hop:
-                @pl.when(z == hop)
-                def _():
-                    right(j, c)
-
-                @pl.when(z == last - hop)
-                def _():
-                    left(last - j, c)
+        j, c = ORDER[k]
+
+        @pl.when(z == hop)
+        def _():
+            right(j, c)
+
+        @pl.when(z == last - hop)
+        def _():
+            left(last - j, c)
 
     def finish(c):
         part = rows_of(c)
@@ -328,16 +326,21 @@
             to_left(z, c).wait_recv()
             gathered[0, part] = gathered[0, part] + from_right[z, part]
 
-        first_hop(functools.partial(y_copy, c))
-
-    def y_second(c):
-        second_hop(functools.partial(y_copy, c), functools.partial(y_wait, c))
-
-    def y_third(c):
-        third_hop(functools.partial(y_copy, c), functools.partial(y_wait, c))
+        if c == len(SPAN) - 1:
+            for k, dom in enumerate((diag, away[3], x_next, y_next, away[1], away[2], sib)):
+                go(y_copy(c, me, dom, k))
+        else:
+            for k, dom in enumerate((diag, x_next, y_next, sib)):
+                go(y_copy(c, me, dom, k))
+
+    def pass_on(c):
+        for k, dom in enumerate((x_next, y_next, diag)):
+            y_wait(c, dom)
+            go(y_copy(c, dom, sib, 4 + k))
 
     def y_split(c):
-        for dom in away:
+        others = (x_next, y_next, diag) if c == len(SPAN) - 1 else ()
+        for dom in (*away, *others):
             y_wait(c, dom)
         first, count = SPAN[c]
         for d in range(doms):
@@ -379,12 +382,38 @@
         spread[d, :, LANES:] = hot.astype(b16)
         pick[d] = jnp.transpose(hot).astype(b16)
 
+    agenda, late = [], []
+    arrival, clock = {}, FIRST
+    for k, (j, c) in enumerate(ORDER):
+        clock += LINK * SPAN[c][1]
+        arrival[j, c, 1] = clock
+        for hop in range(1, j):
+            agenda.append((arrival[j, c, hop] + STOP, relay, (k, hop)))
+            arrival[j, c, hop + 1] = arrival[j, c, hop] + STOP + LINK * SPAN[c][1] + HOP
+    for c, (first, count) in enumerate(SPAN):
+        done = max(arrival[1, c, 1], arrival[2, c, 2], arrival[3, c, 3]) + 2 * STOP
+        agenda.append((done, finish, (c,)))
+        done += 2 * LINK * count + HOP + 1.0
+        if c < len(SPAN) - 1:
+            agenda.append((done, pass_on, (c,)))
+        agenda.append((done + 2.0, y_split, (c,)))
+        if c >= len(SPAN) - 3:
+            late.append(agenda.pop())
+            if c == len(SPAN) - 2:
+                late.insert(0, agenda.pop())
+    agenda.sort(key=lambda item: item[0])
+
+    def tick(now):
+        while agenda and agenda[0][0] <= now:
+            _, act, details = agenda.pop(0)
+            act(*details)
+
     pieces[...] = jnp.zeros_like(pieces)
     ghosts[...] = jnp.zeros_like(ghosts)
     eye = jnp.where(
         lax.broadcasted_iota(jnp.int32, (owned, owned), 0) == lax.broadcasted_iota(jnp.int32, (owned, owned), 1),
         1.0, 0.0)
-    even[0] = eye
+    even[:owned] = eye
     pieces[0, :owned] = eye.astype(b16)
     pieces[0, size : size + owned] = eye.astype(b16)
     prepare(0)
@@ -395,31 +424,35 @@
     for wait in waits:
         wait(sib)
     ready(sib)
-    relay(0)
+    tick(READY - 11.0)
     second_hop(copies[0], waits[0])
-    relay(1)
+    tick(READY - 9.0)
     second_hop(copies[1], waits[1])
     ready(x_next)
     ready(y_next)
+    tick(READY - 6.0)
     third_hop(copies[0], waits[0])
-    relay(2)
     for dom in away[1:3]:
         for wait in waits:
             wait(dom)
         ready(dom)
     third_hop(copies[1], waits[1])
     ready(diag)
-    relay(3)
+    tick(READY - 2.0)
     for wait in waits:
         wait(away[3])
     ready(away[3])
-    finish(0)
 
     every = list(range(doms))
     held = [[0], [6, 7, 0, 1, 2]]
     busy = [[7, 0, 1], [5, 6, 7, 0, 1, 2, 3]]
 
-    def advance(k, middle=()):
+    now = [READY]
+
+    def spend(time):
+        now[0] += time
+
+    def advance(k):
         end = k == DEGREE
         source = held[k - 1] if k <= 2 else every
         active = busy[k - 1] if k <= 2 else every
@@ -433,6 +466,7 @@
                 for base in bases:
                     pieces[after, base + owned : base + owned + slots] = g[:slots]
                     pieces[ahead, base + owned + slots : base + size] = g[slots:]
+        spend(0.05 * len(source))
         for d in active:
             after, ahead = (d + 1) % doms, (d - 1) % doms
             y = mm(matrix[d], pieces[d])
@@ -442,64 +476,47 @@
             ghosts[ahead, 2 * slots : 3 * slots] = low[:slots]
             ghosts[after, slots : 2 * slots] = high[slots:]
             ghosts[after, 3 * slots :] = low[slots:]
-        for act, c in middle:
-            act(c)
+            spend(0.28)
+            if d in STOPS:
+                tick(now[0])
         for d in result:
+            home = slice(d * owned, (d + 1) * owned)
             y = mm(spread[d], ghosts[d])
             if d in active:
                 y = y + image[d]
             v = y if k == 1 else 2.0 * y
             if d in old:
-                v = v - store[d]
+                v = v - store[home]
             if end:
                 for first, count in SPAN:
                     at = doms * first + d * count
-                    odd[at // owned, at % owned : at % owned + count] = v[first : first + count]
+                    odd[at : at + count] = v[first : first + count]
             else:
-                store[d] = v
+                store[home] = v
                 high, low = high_low(v)
                 pieces[d, :owned] = high
                 pieces[d, size : size + owned] = high
                 pieces[d, 2 * size : 2 * size + owned] = low
-
-    advance(1)
-    advance(2, [(relay, 4)])
-    y_second(0)
-    advance(3, [(relay, 5)])
-    y_third(0)
-    advance(4, [(relay, 6)])
-    relay(7)
-    finish(1)
-    advance(5, [(relay, 8)])
-    y_split(0)
-    advance(6, [(relay, 9), (y_second, 1)])
-    relay(10)
-    finish(2)
-    advance(7, [(relay, 11), (y_third, 1)])
-    relay(12)
-    advance(8, [(y_second, 2), (relay, 13), (finish, 3)])
-    relay(14)
-    finish(4)
-    y_third(2)
-    y_split(1)
-    y_second(3)
+        spend(0.055 * len(result))
+
+    for k in range(1, DEGREE + 1):
+        advance(k)
+    tick(1000.0)
     for d in range(doms):
-        high, low = high_low(jnp.transpose(odd[d]))
+        high, low = high_low(jnp.transpose(odd[d * owned : (d + 1) * owned]))
         p_high[:, d * owned : (d + 1) * owned] = high
         p_low[:, d * owned : (d + 1) * owned] = low
-    y_second(4)
-    y_split(2)
-    y_third(3)
-    y_third(4)
-    y_split(3)
 
     def product(at):
         high, low = y_high[at], y_low[at]
         return mm(p_high[:, at], high) + (mm(p_high[:, at], low) + mm(p_low[:, at], high))
 
-    bulk = doms * SPAN[-1][0]
+    bulk = doms * SPAN[-2][0]
+    for _, act, details in late[:2]:
+        act(*details)
     out[...] = product(slice(0, bulk))
-    y_split(4)
+    for _, act, details in late[2:]:
+        act(*details)
     out[...] = out[...] + product(slice(bulk, doms * owned))
 
     for copy in unsent:
@@ -546,8 +563,8 @@
             pltpu.VMEM((doms, 3 * size, owned), b16),
             pltpu.VMEM((doms, 4 * slots, owned), b16),
             pltpu.VMEM((doms, owned, owned), f32),
-            pltpu.VMEM((doms, owned, owned), f32),
-            pltpu.VMEM((doms, owned, owned), f32),
+            pltpu.VMEM((doms * owned, owned), f32),
+            pltpu.VMEM((doms * owned, owned), f32),
             pltpu.VMEM((doms, owned, width), f32),
             pltpu.VMEM((doms * owned, width), b16),
             pltpu.VMEM((doms * owned, width), b16),

time: 64.6 us -> 57.3 us (0.89)
  Pallas kernels: 62.1 us -> 55.2 us
    pallas_call x1, Pallas kernels: 62.1 us -> 55.2 us  [fused(): pl.pallas_call(functools.partial(fused_kernel, bands, owned, slots), out_...]
where the time goes in v3:
time: 57.3 us; the launch traced here: 57.1 us
  Pallas kernels  55.2 us (96%)
  local copies, waits for them, and re-layouts  1.87 us (3%)
    pallas_call x1, Pallas kernels, fused(): pl.pallas_call(functools.partial(fused_kernel, bands, owned, slots), out_...  55.2 us
    unnamed x1, local copies, waits for them, and re-layouts  1.87 us

profile of v3, /device:TPU:17, one launch (start us, length us, event | category | flops | bytes accessed | tf_op | source)
XLA Modules:
  0.0 57.1 jit_solution(16706156399791459174)
XLA Ops:
  0.0 55.2 %shard_map.55 = f32[256,512]{1,0:T(8,128)} custom-call(f32[256,512]{1,0:T(8,128)} %waves_in.1, f32[125,8,125]{2,1,0:T(8,128)} %bitcast.1, s32[8,125]{1,0:T(8,128)} %conn.1, s32[1,2,64]{2,1,0:T(2,128)} %send.1, f32[512,2048]{1,0:T(8,128)} %rotation_in.1), custom_call_target="tpu_custom_call" | custom-call | flops 14495514624 | bytes 16777216 | tf_op jit(solution)/shard_map/pallas_call | solution.py:546
  55.2 1.9 %copy.7 = f32[256,512]{1,0:T(8,128)} copy(f32[256,512]{1,0:T(8,128)} %shard_map.55) | data formatting | bytes 1048576

commit v4 on v3

--- a/solution.py
+++ b/solution.py
@@ -11,11 +11,12 @@
 LANES = 128
 MESH = pl.DeviceIdType.MESH
 SPAN = ((0, 96), (96, 64), (160, 48), (208, 32), (240, 16))
-ORDER = ((3, 0), (2, 0), (3, 1), (1, 0), (3, 2), (2, 1), (1, 1), (3, 3), (2, 2), (1, 2), (3, 4), (2, 3), (2, 4),
+ORDER = ((3, 0), (3, 1), (2, 0), (1, 0), (3, 2), (2, 1), (1, 1), (3, 3), (2, 2), (1, 2), (3, 4), (2, 3), (2, 4),
          (1, 3), (1, 4))
-FIRST, LINK, HOP, STOP, READY = 4.2, 2.8 / 64, 1.7, 0.2, 22.0
+FIRST, LINK, HOP, STOP, READY = 4.4, 2.8 / 64, 1.7, 0.2, 21.0
 STOPS = (3, 7)
-HALVES = ((0, 104), (104, 96))
+CLOSE = (1, 3, 5, 7)
+HALVES = ((0, 136), (136, 64))
 
 
 centre = 5.5
@@ -192,20 +193,23 @@
     beside = lax.div(z + bands - 1, bands) + lax.div(2 * bands - 2 - z, bands)
     pl.semaphore_wait(barrier, doms - 1 + beside)
 
-    send_right(ORDER[:1])
-    send_left(ORDER[:1])
+    send_right(ORDER[:2])
+    send_left(ORDER[:2])
 
     loads[3].wait()
     node = lax.broadcasted_iota(jnp.int32, (size, conn.shape[1]), 0)
-    total = jnp.zeros((size, size), jnp.float32)
+    stacks = [[], [], []]
+    gap = jnp.zeros((size, LANES - conn.shape[1]), b16)
     for c in range(cells.shape[1]):
         seat = jnp.where(node == conn[c : c + 1, :], 1.0, 0.0).astype(b16)
         a_high, a_low = high_low(cells[:, c, :])
         b_high, b_low = high_low(mm(seat, a_high) + mm(seat, a_low))
-        dims = (((1,), (1,)), ((), ()))
-        total = total + (
-            lax.dot_general(b_high, seat, dims, preferred_element_type=jnp.float32)
-            + lax.dot_general(b_low, seat, dims, preferred_element_type=jnp.float32))
+        for stack, part in zip(stacks, (b_high, b_low, seat)):
+            stack += [part, gap]
+    b_high, b_low, seats = (jnp.concatenate(stack, axis=1) for stack in stacks)
+    dims = (((1,), (1,)), ((), ()))
+    total = lax.dot_general(b_high, seats, dims, preferred_element_type=jnp.float32) + lax.dot_general(
+        b_low, seats, dims, preferred_element_type=jnp.float32)
     r_at = lax.broadcasted_iota(jnp.int32, (size, size), 0)
     c_at = lax.broadcasted_iota(jnp.int32, (size, size), 1)
     shift = jnp.where((r_at == c_at) & (r_at < owned), centre, 0.0)
@@ -287,8 +291,8 @@
         copy.wait()
     partial(2)
     partial(1)
-    send_right(ORDER[1:])
-    send_left(ORDER[1:])
+    send_right(ORDER[2:])
+    send_left(ORDER[2:])
 
     def relay(k, hop):
         def right(j, c):
@@ -391,7 +395,7 @@
             agenda.append((arrival[j, c, hop] + STOP, relay, (k, hop)))
             arrival[j, c, hop + 1] = arrival[j, c, hop] + STOP + LINK * SPAN[c][1] + HOP
     for c, (first, count) in enumerate(SPAN):
-        done = max(arrival[1, c, 1], arrival[2, c, 2], arrival[3, c, 3]) + 2 * STOP
+        done = max(arrival[1, c, 1], arrival[2, c, 2], arrival[3, c, 3]) + (2 * STOP if c else 2.0)
         agenda.append((done, finish, (c,)))
         done += 2 * LINK * count + HOP + 1.0
         if c < len(SPAN) - 1:
@@ -436,6 +440,7 @@
         for wait in waits:
             wait(dom)
         ready(dom)
+    tick(READY - 4.0)
     third_hop(copies[1], waits[1])
     ready(diag)
     tick(READY - 2.0)
@@ -469,15 +474,21 @@
         spend(0.05 * len(source))
         for d in active:
             after, ahead = (d + 1) % doms, (d - 1) % doms
-            y = mm(matrix[d], pieces[d])
+            if k > 1:
+                y = mm(matrix[d], pieces[d])
+            elif d == 0:
+                y = matrix[d, :, :owned].astype(jnp.float32) + matrix[d, :, size : size + owned].astype(jnp.float32)
+            else:
+                beyond = pieces[d, owned:size]
+                y = mm(matrix[d, :, owned:size], beyond) + mm(matrix[d, :, size + owned : 2 * size], beyond)
             image[d] = y[:owned]
             high, low = high_low(y[owned:])
             ghosts[ahead, :slots] = high[:slots]
             ghosts[ahead, 2 * slots : 3 * slots] = low[:slots]
             ghosts[after, slots : 2 * slots] = high[slots:]
             ghosts[after, 3 * slots :] = low[slots:]
-            spend(0.28)
-            if d in STOPS:
+            spend(0.28 if k > 1 else 0.1)
+            if d in (CLOSE if k >= DEGREE - 1 else STOPS):
                 tick(now[0])
         for d in result:
             home = slice(d * owned, (d + 1) * owned)

time: 57.3 us -> 56.2 us (0.981); the launches traced: 57.1 us -> 55.1 us
  Pallas kernels: 55.2 us -> 53.2 us
    pallas_call x1, Pallas kernels: 55.2 us -> 53.2 us  [fused(): pl.pallas_call(functools.partial(fused_kernel, bands, owned, slots), out_...]
where the time goes in v4:
time: 56.2 us; the launch traced here: 55.1 us
  Pallas kernels  53.2 us (95%)
  local copies, waits for them, and re-layouts  1.87 us (3%)
    pallas_call x1, Pallas kernels, fused(): pl.pallas_call(functools.partial(fused_kernel, bands, owned, slots), out_...  53.2 us
    unnamed x1, local copies, waits for them, and re-layouts  1.87 us

profile of v4, /device:TPU:17, one launch (start us, length us, event | category | flops | bytes accessed | tf_op | source)
XLA Modules:
  0.0 55.1 jit_solution(5242387350355582763)
XLA Ops:
  0.0 53.2 %shard_map.55 = f32[256,512]{1,0:T(8,128)} custom-call(f32[256,512]{1,0:T(8,128)} %waves_in.1, f32[125,8,125]{2,1,0:T(8,128)} %bitcast.1, s32[8,125]{1,0:T(8,128)} %conn.1, s32[1,2,64]{2,1,0:T(2,128)} %send.1, f32[512,2048]{1,0:T(8,128)} %rotation_in.1), custom_call_target="tpu_custom_call" | custom-call | flops 14495514624 | bytes 16777216 | tf_op jit(solution)/shard_map/pallas_call | solution.py:557
  53.2 1.9 %copy.7 = f32[256,512]{1,0:T(8,128)} copy(f32[256,512]{1,0:T(8,128)} %shard_map.55) | data formatting | bytes 1048576

commit v5 on v4

--- a/solution.py
+++ b/solution.py
@@ -15,8 +15,8 @@
          (1, 3), (1, 4))
 FIRST, LINK, HOP, STOP, READY = 4.4, 2.8 / 64, 1.7, 0.2, 21.0
 STOPS = (3, 7)
-CLOSE = (1, 3, 5, 7)
-HALVES = ((0, 136), (136, 64))
+CLOSE = (0, 2, 4, 6, 7)
+HALVES = ((0, 152), (152, 48))
 
 
 centre = 5.5

time: 56.2 us -> 57 us (1.014)
  the two profiles are of different devices: /device:TPU:17 before, /device:TPU:0 now
where the time goes in v5:
time: 57 us; the launch traced here: 56.8 us
  Pallas kernels  55 us (96%)
  local copies, waits for them, and re-layouts  1.87 us (3%)
    pallas_call x1, Pallas kernels, fused(): pl.pallas_call(functools.partial(fused_kernel, bands, owned, slots), out_...  55 us
    unnamed x1, local copies, waits for them, and re-layouts  1.87 us

profile of v5, /device:TPU:0, one launch (start us, length us, event | category | flops | bytes accessed | tf_op | source)
XLA Modules:
  0.0 56.8 jit_solution(5483308495394452677)
XLA Ops:
  0.0 55.0 %shard_map.55 = f32[256,512]{1,0:T(8,128)} custom-call(f32[256,512]{1,0:T(8,128)} %waves_in.1, f32[125,8,125]{2,1,0:T(8,128)} %bitcast.1, s32[8,125]{1,0:T(8,128)} %conn.1, s32[1,2,64]{2,1,0:T(2,128)} %send.1, f32[512,2048]{1,0:T(8,128)} %rotation_in.1), custom_call_target="tpu_custom_call" | custom-call | flops 14495514624 | bytes 16777216 | tf_op jit(solution)/shard_map/pallas_call | solution.py:557
  55.0 1.9 %copy.7 = f32[256,512]{1,0:T(8,128)} copy(f32[256,512]{1,0:T(8,128)} %shard_map.55) | data formatting | bytes 1048576
